TPU v7x, 32 devices: a whole 2x2x4 slice. The times are simulated.
32 devices in a mesh: wave: 8 (over z, x), lev: 4 (over y, core).
Axes of the slice: x: 2, y: 2, z: 4, core: 2. Of those that a mesh axis runs over, the one named last changes fastest.
Arguments:
- spectral: bfloat16 [24, 128, 1280], P('lev', 'wave'), may hold values from -0.19921875 to 0.19921875
- legendre: bfloat16 [128, 32, 1280], P('wave', 'lev'), may hold values from -0.15625 to 0.15625
- weights: float32 [32], replicated, may hold values from 4 to 40
- nlon: int32 [32], replicated, may hold values from 20 to 5136, as said below
- assignment: int32 [128], replicated, may hold values from 1 to 1279, as said below
Outputs:
- tendencies: float32 [24, 128, 1280], P('lev', 'wave')
Inputs may be any that keep to these rules, and one draw needn't show every extreme that they name: `assignment`: slots 2 i and 2 i + 1 hold m and 1280 - m for some m with 1 <= m < 640; all values are distinct, and m = 1 is always among them. `nlon`: each count is 20 plus four times a whole number; both ends of the range occur in every draw.
All inputs are finite; a program needn't handle non-finite values.
Results may differ from a plain program's by a relative error of at most 0.018.
Values may be sent and summed in bfloat16 or wider, within the bound.
A program may use at most 64 MiB of HBM per device.

v0:
```python
import math

import jax
import jax.numpy as jnp
from jax import lax
from jax.sharding import PartitionSpec as P

TRUNC = 1279
LON_BLOCK = 768
NLONPAD = 5376


def angle_parts(count, waves, starts):
    phase = starts[:, None] % count * waves[None, :] % count
    angle = 2.0 * math.pi * phase.astype(jnp.float32) / count.astype(jnp.float32)
    return (jnp.cos(angle), jnp.sin(angle))


def compose_table(count, waves, coarse_cos, coarse_sin, fine_cos, fine_sin, lon_rows):
    cosine = (
        coarse_cos[:, None, :] * fine_cos[None, :, :]
        - coarse_sin[:, None, :] * fine_sin[None, :, :]
    )
    sine = (
        coarse_sin[:, None, :] * fine_cos[None, :, :]
        + coarse_cos[:, None, :] * fine_sin[None, :, :]
    )
    rows_total = lon_rows.shape[0]
    cosine = cosine.reshape(rows_total, waves.shape[0])
    sine = sine.reshape(rows_total, waves.shape[0])
    usable = (lon_rows[:, None] < count) & (2 * waves[None, :] < count)
    cosine = jnp.where(usable, cosine, jnp.zeros((), jnp.float32))
    sine = jnp.where(usable, -sine, jnp.zeros((), jnp.float32))
    return jnp.concatenate([cosine, sine], axis=1).astype(jnp.bfloat16)


def quadratic(grid):
    fields = grid.reshape(grid.shape[0], grid.shape[1] // 3, 3)
    vort = fields[:, :, 0]
    diverg = fields[:, :, 1]
    temper = fields[:, :, 2]
    stacked = jnp.stack([vort * temper, diverg * temper, vort * diverg], axis=-1)
    return stacked.reshape(grid.shape[0], grid.shape[1]).astype(jnp.bfloat16)


def per_device(spectral, legendre, weights, nlon, assignment):
    wave_index = lax.axis_index("wave")
    lev_index = lax.axis_index("lev")
    slots = legendre.shape[0]
    lat_band = legendre.shape[1]
    kmax_width = legendre.shape[2]
    all_slots = assignment.shape[0]
    own_waves = lax.dynamic_slice_in_dim(assignment, wave_index * slots, slots)
    krange = lax.iota(jnp.int32, kmax_width)
    live_rows = krange[None, :] <= (TRUNC - own_waves)[:, None]
    local = jnp.where(live_rows[None], spectral, jnp.zeros((), jnp.bfloat16))
    spec_all = lax.all_gather(local, "lev", axis=0, tiled=True)
    columns = spec_all.shape[0]
    four_local = jnp.einsum(
        "mlk,cmk->mlc", legendre, spec_all, preferred_element_type=jnp.float32
    ).astype(jnp.bfloat16)
    fourier = lax.all_to_all(four_local, "wave", split_axis=1, concat_axis=0, tiled=True)
    mine = fourier.shape[1]
    half_cols = columns // 2
    fine_rows = lax.iota(jnp.int32, 128)
    coarse_rows = lax.iota(jnp.int32, NLONPAD // 128) * 128
    coarse_step = LON_BLOCK // 128
    lat_index = lev_index * lat_band + wave_index * mine + 0
    count = lax.dynamic_slice_in_dim(nlon, lat_index, 1)[0]
    weight = lax.dynamic_slice_in_dim(weights, lat_index, 1)[0]
    pairs = fourier[:, 0, :].reshape(all_slots, half_cols, 2)
    stacked = jnp.concatenate([pairs[:, :, 0], pairs[:, :, 1]], axis=0)
    fine_cos, fine_sin = angle_parts(count, assignment, fine_rows)
    coarse_cos_all, coarse_sin_all = angle_parts(count, assignment, coarse_rows)

    def lon_block(block_step, total):
        lon_rows = block_step * LON_BLOCK + lax.iota(jnp.int32, LON_BLOCK)
        coarse_cos = lax.dynamic_slice_in_dim(coarse_cos_all, block_step * coarse_step, coarse_step)
        coarse_sin = lax.dynamic_slice_in_dim(coarse_sin_all, block_step * coarse_step, coarse_step)
        table = compose_table(
            count, assignment, coarse_cos, coarse_sin, fine_cos, fine_sin, lon_rows
        )
        grid = 2.0 * jnp.dot(table, stacked, preferred_element_type=jnp.float32)
        products = quadratic(grid)
        return total + lax.dot_general(
            table, products, (((0,), (0,)), ((), ())), preferred_element_type=jnp.float32
        )

    start_total = jnp.zeros((2 * all_slots, half_cols), jnp.float32)
    total = lax.fori_loop(0, NLONPAD // LON_BLOCK, lon_block, start_total)
    back = total * (weight / count.astype(jnp.float32))
    joined = jnp.stack([back[:all_slots], back[all_slots:]], axis=-1).reshape(all_slots, columns)
    analysed_rows = [joined.astype(jnp.bfloat16)]
    analysed = jnp.stack(analysed_rows, axis=1)
    returned = lax.all_to_all(analysed, "wave", split_axis=0, concat_axis=1, tiled=True)
    band_term = jnp.einsum("mlc,mlk->cmk", returned, legendre, preferred_element_type=jnp.float32)
    band_term = jnp.where(live_rows[None], band_term, jnp.zeros((), jnp.float32))
    return lax.psum_scatter(
        band_term.astype(jnp.bfloat16), "lev", scatter_dimension=0, tiled=True
    ).astype(jnp.float32)


def solution(mesh):
    return jax.shard_map(
        per_device,
        mesh=mesh,
        in_specs=(P("lev", "wave", None), P("wave", "lev", None), P(), P(), P()),
        out_specs=P("lev", "wave", None),
        check_vma=False,
    )
```

profile of v0, /device:TPU:0, one launch (start us, length us, event | category | flops | bytes accessed | tf_op | source)
XLA Modules:
  0.0 98.4 jit_solution(2222853748882733993)
XLA Ops:
  6.5 0.8 dynamic-slice_subtract_fusion
  7.4 1.0 broadcast_select_fusion
  8.4 11.1 %all_gather.3 = bf16[24,16,1280]{2,1,0:T(8,128)(2,1)S(1)} all-gather(bf16[6,16,1280]{2,1,0:T(8,128)(2,1)S(1)} %broadcast_select_fusion), channel_id=1, replica_groups=mesh['wave'=8,'lev'=4] {'lev'}, dimensions={0}, use_global_device_ids=true | all-gather | bytes 1228800 | tf_op jit(solution)/shard_map/all_gather | solution.py:57
  19.5 0.4 fusion.19
  19.9 0.7 reshape.139
  20.7 5.8 %all-to-all-start = ((bf16[8,2,192]{2,1,0:T(2,128)(2,1)}), bf16[8,2,192]{2,1,0:T(2,128)(2,1)S(1)}, u32[]{:S(2)}, u32[]{:S(2)}) async-start(bf16[8,2,192]{2,1,0:T(2,128)(2,1)} %reshape.139), calls=%async_computation | async-start | bytes 16384 | tf_op jit(solution)/shard_map/all_to_all | solution.py:62
  26.5 0.6 dynamic_slice.24
  28.8 0.1 and_select_fusion.3
  28.9 0.4 fusion.30
  29.4 0.1 and_select_fusion.2
  29.5 0.7 dynamic_slice.25
  30.9 2.1 %all-to-all-done = bf16[8,2,192]{2,1,0:T(2,128)(2,1)S(1)} async-done(((bf16[8,2,192]{2,1,0:T(2,128)(2,1)}), bf16[8,2,192]{2,1,0:T(2,128)(2,1)S(1)}, u32[]{:S(2)}, u32[]{:S(2)}) %all-to-all-start) | async-done | bytes 6176 | tf_op jit(solution)/shard_map/all_to_all | solution.py:62
  33.3 21.5 %while.16 = (s32[]{:T(128)}, f32[256,12]{0,1:T(8,128)S(1)}, s32[]{:T(128)}, s32[128]{0:T(128)S(1)}, f32[42,128]{1,0:T(8,128)S(1)}, /*index=5*/f32[42,128]{1,0:T(...) while((s32[]{:T(128)}, f32[256,12]{0,1:T(8,128)S(1)}, ...), condition=%wide.region_1.2_spmd.clone.clone.clone, body=%wide.region_0.1_spmd.clone.clone.clone.sunk | while | flops 12460808 | bytes 2539002 | solution.py:90
  33.4 0.6 multiply_compare_fusion.2
  33.9 0.6 add_compare_fusion.2
  34.5 1.0 fusion.43
  35.5 0.1 multiply_subtract_fusion.2
  35.6 0.2 fusion.44
  35.8 0.2 convolution_multiply_fusion.2
  36.2 0.1 convolution_add_fusion.2
  36.4 0.6 multiply_compare_fusion.2
  37.0 0.6 add_compare_fusion.2
  37.6 1.0 fusion.43
  38.7 0.2 fusion.44
  38.9 0.2 convolution_multiply_fusion.2
  39.3 0.1 convolution_add_fusion.2
  39.5 0.6 multiply_compare_fusion.2
  40.1 0.6 add_compare_fusion.2
  40.7 1.0 fusion.43
  41.8 0.2 fusion.44
  42.0 0.2 convolution_multiply_fusion.2
  42.4 0.1 convolution_add_fusion.2
  42.5 0.6 multiply_compare_fusion.2
  43.1 0.6 add_compare_fusion.2
  43.7 1.0 fusion.43
  44.7 0.1 multiply_subtract_fusion.2
  44.9 0.2 fusion.44
  45.0 0.2 convolution_multiply_fusion.2
  45.5 0.1 convolution_add_fusion.2
  45.6 0.6 multiply_compare_fusion.2
  46.2 0.6 add_compare_fusion.2
  46.8 1.0 fusion.43
  47.9 0.2 fusion.44
  48.1 0.2 convolution_multiply_fusion.2
  48.5 0.1 convolution_add_fusion.2
  48.7 0.6 multiply_compare_fusion.2
  49.3 0.6 add_compare_fusion.2
  49.9 1.0 fusion.43
  51.0 0.2 fusion.44
  51.2 0.2 convolution_multiply_fusion.2
  51.6 0.1 convolution_add_fusion.2
  51.7 0.6 multiply_compare_fusion.2
  52.4 0.6 add_compare_fusion.2
  53.0 1.0 fusion.43
  54.1 0.2 fusion.44
  54.3 0.2 convolution_multiply_fusion.2
  54.7 0.1 convolution_add_fusion.2
  54.9 0.5 broadcast.166
  55.4 0.6 reduce
  56.3 10.2 %all_to_all.33 = bf16[8,2,192]{2,1,0:T(2,128)(2,1)S(1)} all-to-all(bf16[8,2,192]{2,1,0:T(2,128)(2,1)S(1)} %reshape.141), channel_id=1, replica_groups=mesh['wave'=8,'lev'=4] {'wave'}, dimensions={0} | all-to-all | bytes 12288 | tf_op jit(solution)/shard_map/all_to_all | solution.py:95
  66.6 0.5 fusion.18
  67.1 1.1 %copy.31 = bf16[24,16,1280]{2,1,0:T(8,128)(2,1)} copy(bf16[24,16,1280]{2,0,1:T(8,128)(2,1)S(1)} %fusion.18) | data formatting | bytes 1966080 | tf_op jit(solution)/shard_map/convert_element_type | solution.py:99
  68.2 21.5 %reduce-scatter.2.cloned.1.call-done = bf16[6,16,1280]{2,1,0:T(8,128)(2,1)} async-done(((bf16[24,16,1280]{2,1,0:T(8,128)(2,1)}), bf16[6,16,1280]{2,1,0:T(8,128)(2,1)}) %reduce-scatter.2.cloned.1.call-update) | async-done | bytes 245776 | tf_op jit(solution)/shard_map/reduce_scatter | solution.py:98
  89.8 1.8 %convert_element_type.58 = f32[6,16,1280]{2,1,0:T(8,128)} convert(bf16[6,16,1280]{2,1,0:T(8,128)(2,1)} %reduce-scatter.2.cloned.1.call-done) | non-fusion elementwise | flops 122880 | bytes 737280 | tf_op jit(solution)/shard_map/convert_element_type | solution.py:100
  (68 shorter events, 2.7 us)
Async XLA Ops:
  6.5 13.0 %copy-start = (bf16[16,8,1280]{2,1,0:T(8,128)(2,1)S(1)}, bf16[16,8,1280]{2,1,0:T(8,128)(2,1)}, u32[]{:S(2)}) copy-start(bf16[16,8,1280]{2,1,0:T(8,128)(2,1)} %param.8) | copy-start | bytes 983044
  19.5 7.0 %copy-start.2 = (s32[32]{0:T(128)S(1)}, s32[32]{0:T(128)}, u32[]{:S(2)}) copy-start(s32[32]{0:T(128)} %param.10) | copy-start | bytes 388
  19.5 9.4 %copy-start.1 = (s32[128]{0:T(128)S(1)}, s32[128]{0:T(128)}, u32[]{:S(2)}) copy-start(s32[128]{0:T(128)} %param.11) | copy-start | bytes 1540
  19.5 10.0 %copy-start.3 = (f32[32]{0:T(128)S(1)}, f32[32]{0:T(128)}, u32[]{:S(2)}) copy-start(f32[32]{0:T(128)} %param.9) | copy-start | bytes 388
  20.7 12.3 %all-to-all-start = ((bf16[8,2,192]{2,1,0:T(2,128)(2,1)}), bf16[8,2,192]{2,1,0:T(2,128)(2,1)S(1)}, u32[]{:S(2)}, u32[]{:S(2)}) async-start(bf16[8,2,192]{2,1,0:T(2,128)(2,1)} %reshape.139), calls=%async_computation | async-start | bytes 16384 | tf_op jit(solution)/shard_map/all_to_all | solution.py:62
  26.5 63.3 %reduce-scatter.2.cloned.1.call-start = ((), (), s32[]{:S(2)}) async-start(), calls=%async_computation.3 | async-start | bytes 1228800 | tf_op jit(solution)/shard_map/reduce_scatter | solution.py:98
Sparse Core Ops, SparseCore 0:
  68.4 21.3 reduce-scatter.1
where the time goes:
time: 98.8 us; the launch traced here: 98.4 us
  waiting for transfers between devices  23.6 us (24%)
  other arithmetic  22.7 us (23%)
  blocking collectives  21.3 us (22%)
  between operations  16 us (16%)
  starting transfers between devices  5.84 us (6%)
  local copies, waits for them, and re-layouts  4.94 us (5%)
  matrix products  3.42 us (3%)
    reduce_scatter x1, waiting for transfers between devices, per_device(): lax.psum_scatter(band_term.astype(jnp.bfloat16), 'lev', scatter_dimension...  21.5 us
    all_gather x1, blocking collectives, per_device(): spec_all = lax.all_gather(local, 'lev', axis=0, tiled=True)  11.1 us
    all_to_all x1, blocking collectives, per_device(): lax.all_to_all(analysed, 'wave', split_axis=0, concat_axis=1, tiled=True)  10.2 us
    lt x14, other arithmetic, compose_table(): usable = (lon_rows[:, None] < count) & (2 * waves[None, :] < count)  8.18 us
    cos x7, other arithmetic, angle_parts(): return (jnp.cos(angle), jnp.sin(angle))  6.88 us
    all_to_all x1, starting transfers between devices, per_device(): lax.all_to_all(four_local, 'wave', split_axis=1, concat_axis=0, tiled=True)  5.81 us
    all_to_all x1, waiting for transfers between devices, per_device(): lax.all_to_all(four_local, 'wave', split_axis=1, concat_axis=0, tiled=True)  2.07 us
  transfers between devices with their start and end apart: 2, of which 2 were waited for; matrix products, arithmetic and copies ran while one was open for 2% of the time, Pallas kernels for 0%

commit v1 on v0

--- a/solution.py
+++ b/solution.py
@@ -1,8 +1,11 @@
+import functools
 import math
 
 import jax
 import jax.numpy as jnp
 from jax import lax
+from jax.experimental import pallas as pl
+from jax.experimental.pallas import tpu as pltpu
 from jax.sharding import PartitionSpec as P
 
 TRUNC = 1279
@@ -100,9 +103,354 @@
     ).astype(jnp.float32)
 
 
+MESH = pl.DeviceIdType.MESH
+LANE = 128
+F32, BF16, I32 = jnp.float32, jnp.bfloat16, jnp.int32
+NT = (((1,), (1,)), ((), ()))
+NN = (((1,), (0,)), ((), ()))
+
+
+def dot(a, b, dims):
+    return lax.dot_general(a, b, dims, preferred_element_type=F32)
+
+
+def iota(shape, dim):
+    return lax.broadcasted_iota(I32, shape, dim)
+
+
+def fused_kernel(
+    nlon, weights, waves_s, waves_v, spec, leg, out,
+    legp, coefx, tab, rmat, fsend, frecv, bsend, brecv,
+    ag_send, ag_recv, f_ssem, f_rsem, b_ssem, b_rsem,
+):
+    n_wave, n_lev = 8, 4
+    cols, slots, kmax = spec.shape
+    lats = leg.shape[1]
+    blocks = kmax // LANE
+    places = blocks + 1
+    chunks = slots // 4
+    me = lax.axis_index("wave")
+    lev = lax.axis_index("lev")
+    sibling = lev + 1 - 2 * lax.rem(lev, 2)
+    across = lax.rem(lev + 2, n_lev)
+    far = lax.rem(sibling + 2, n_lev)
+
+    def peer(step):
+        return lax.rem(me + step, n_wave)
+
+    barrier = pltpu.get_barrier_semaphore()
+    for step in range(1, n_wave):
+        pl.semaphore_signal(barrier, inc=1, device_id=(peer(step), lev), device_id_type=MESH)
+    for other in (sibling, across):
+        pl.semaphore_signal(barrier, inc=1, device_id=(me, other), device_id_type=MESH)
+
+    def lev_copy(band, chunk, target, sem):
+        return pltpu.make_async_remote_copy(
+            src_ref=legp.at[band, chunk],
+            dst_ref=legp.at[band, chunk],
+            send_sem=ag_send.at[sem, chunk],
+            recv_sem=ag_recv.at[sem, chunk],
+            device_id=(me, target),
+            device_id_type=MESH,
+        )
+
+    own = [waves_s[me * slots + s] for s in range(slots)]
+
+    def pack_chunk(chunk):
+        counts = [
+            (jnp.full((lats, LANE), TRUNC + 1, I32) - own[2 * i] + (LANE - 1)) // LANE
+            for i in (2 * chunk, 2 * chunk + 1)
+        ]
+        for p in range(places):
+            halves = []
+            for h in range(2):
+                i = 2 * chunk + h
+                if p < blocks:
+                    first = leg[2 * i, :, p * LANE:(p + 1) * LANE].astype(F32)
+                if p > 0:
+                    q = blocks - p
+                    second = leg[2 * i + 1, :, q * LANE:(q + 1) * LANE].astype(F32)
+                if p == 0:
+                    halves.append(first)
+                elif p == blocks:
+                    halves.append(second)
+                else:
+                    halves.append(jnp.where(counts[h] > p, first, second))
+            legp[lev, chunk, :, p * LANE:(p + 1) * LANE] = jnp.concatenate(halves, axis=0).astype(BF16)
+
+    for chunk in range(chunks):
+        pack_chunk(chunk)
+        if chunk == 0:
+            pl.semaphore_wait(barrier, n_wave - 1 + 2)
+        lev_copy(lev, chunk, across, 0).start()
+        lev_copy(lev, chunk, sibling, 1).start()
+
+    row16 = iota((slots, LANE), 0)
+    lane16 = iota((slots, LANE), 1)
+    even_row = lax.rem(row16, 2) == 0
+    last = jnp.zeros((slots, LANE), I32)
+    for s in range(slots):
+        last = jnp.where(row16 == s, TRUNC - own[s], last)
+    zero16 = jnp.zeros((slots, LANE), F32)
+    coefx[...] = jnp.zeros(coefx.shape, BF16)
+    rows_at = pl.ds(pl.multiple_of(me * slots, slots), slots)
+    for p in range(places):
+        q = blocks - p
+        live = jnp.where(even_row, p * LANE, q * LANE) + lane16 <= last
+        for c in range(cols):
+            even = spec[c, :, p * LANE:(p + 1) * LANE].astype(F32) if p < blocks else zero16
+            odd = spec[c, :, q * LANE:(q + 1) * LANE].astype(F32) if p > 0 else zero16
+            value = jnp.where(live, jnp.where(even_row, even, odd), 0.0)
+            coefx[c, rows_at, p * LANE:(p + 1) * LANE] = value.astype(BF16)
+
+    waves = waves_v[...]
+    waves_f = waves.astype(F32)
+
+    def forward(chunk):
+        lev_copy(across, chunk, across, 0).wait_recv()
+        lev_copy(across, chunk, sibling, 2).start()
+
+    def tables(b):
+        count = jnp.full((1, LANE), nlon[b * n_wave + me], I32)
+        count_f = count.astype(F32)
+        inverse = 1.0 / count_f
+        row = iota((40, LANE), 0)
+        lon = jnp.where(row < 8, row, jnp.where(row < 24, 8 * (row - 8), LANE * (row - 24)))
+        whole = lon.astype(F32) * waves_f
+        phase = whole - jnp.floor(whole * inverse) * count_f
+        phase = jnp.where(phase < 0.0, phase + count_f, phase)
+        phase = jnp.where(phase >= count_f, phase - count_f, phase)
+        angle = 2.0 * math.pi * phase / count_f
+        cosine, sine = jnp.cos(angle), jnp.sin(angle)
+        usable = 2 * waves < count
+        c8, s8 = cosine[0:8], sine[0:8]
+        fine_cos, fine_sin = [], []
+        for t in range(16):
+            cm, sm = cosine[8 + t:9 + t], sine[8 + t:9 + t]
+            fine_cos.append(cm * c8 - sm * s8)
+            fine_sin.append(sm * c8 + cm * s8)
+        fine_cos = jnp.concatenate(fine_cos, axis=0)
+        fine_sin = jnp.concatenate(fine_sin, axis=0)
+        for t in range(tab.shape[1] // LANE):
+            cq = jnp.where(usable, cosine[24 + t:25 + t], 0.0)
+            sq = jnp.where(usable, sine[24 + t:25 + t], 0.0)
+            tab[b, t * LANE:(t + 1) * LANE, 0:LANE] = (cq * fine_cos - sq * fine_sin).astype(BF16)
+            tab[b, t * LANE:(t + 1) * LANE, LANE:2 * LANE] = (-(sq * fine_cos + cq * fine_sin)).astype(BF16)
+
+    for b in range(n_lev):
+        tables(b)
+        forward(b)
+
+    depth = n_lev * slots // 2 * lats
+    rrow = iota((depth, depth), 0)
+    rcol = iota((depth, depth), 1)
+    band_c = rcol // (slots // 2 * lats)
+    same = (rrow // 32) == lax.rem(rcol, lats)
+    base = (band_c // 2) * 16 + lax.rem(band_c, 2) * 4
+    for c in range(cols):
+        hit = same & (lax.rem(rrow, 32) == base + (c % 2) * 8 + (2 - c // 2))
+        rmat[:, c * depth:(c + 1) * depth] = jnp.where(hit, 1.0, 0.0).astype(BF16)
+
+    half = slots // 2 * lats
+    coef_all = coefx[...].reshape(cols * LANE, places * LANE)
+    yrow = iota((half, LANE), 0) // lats
+    ylane = iota((half, LANE), 1)
+    mine = (ylane // slots == me) & (lax.rem(ylane, slots) // 2 == yrow)
+    srow = iota((n_wave * 8, half), 0)
+    scol = iota((n_wave * 8, half), 1)
+    same_lat = srow // 8 == lax.rem(scol, lats)
+
+    def synth(band):
+        packed = legp[band].reshape(half, places * LANE)
+        four = dot(packed, coef_all, NT)
+        pick = jnp.where(same_lat & (lax.rem(srow, 8) == band), 1.0, 0.0).astype(BF16)
+        parts = [
+            jnp.where(mine, four[:, c * LANE:(c + 1) * LANE], 0.0).astype(BF16) for c in range(cols)
+        ]
+        return dot(pick, jnp.concatenate(parts, axis=1), NN)
+
+    total = synth(lev)
+    for chunk in range(chunks):
+        lev_copy(sibling, chunk, sibling, 1).wait_recv()
+    total = total + synth(sibling)
+    total = total + synth(across)
+    for chunk in range(chunks):
+        lev_copy(far, chunk, sibling, 2).wait_recv()
+    total = total + synth(far)
+    for j in range(n_wave):
+        for f in range(cols // 2):
+            fsend[j, f * 16:(f + 1) * 16, :] = jnp.concatenate(
+                [
+                    total[j * 8:(j + 1) * 8, (2 * f) * LANE:(2 * f + 1) * LANE],
+                    total[j * 8:(j + 1) * 8, (2 * f + 1) * LANE:(2 * f + 2) * LANE],
+                ],
+                axis=0,
+            ).astype(BF16)
+
+    def four_copy(step, slot):
+        return pltpu.make_async_remote_copy(
+            src_ref=fsend.at[peer(step)],
+            dst_ref=frecv.at[slot],
+            send_sem=f_ssem.at[step],
+            recv_sem=f_rsem.at[step],
+            device_id=(peer(step), lev),
+            device_id_type=MESH,
+        )
+
+    def back_copy(step, slot):
+        return pltpu.make_async_remote_copy(
+            src_ref=bsend,
+            dst_ref=brecv.at[slot],
+            send_sem=b_ssem.at[step],
+            recv_sem=b_rsem.at[step],
+            device_id=(peer(step), lev),
+            device_id_type=MESH,
+        )
+
+    for step in range(1, n_wave):
+        four_copy(step, me).start()
+    frecv[me] = fsend[me]
+    for step in range(1, n_wave):
+        four_copy(step, peer(n_wave - step)).wait_recv()
+
+    gathered = jnp.sum(frecv[...].astype(F32), axis=0)
+    even_m = lax.rem(waves, 2) == 0
+    row8 = iota((8, LANE), 0)
+    in_pair = lax.rem(row8, 4)
+    nothing = jnp.zeros((8, LANE), F32)
+    width = tab.shape[1]
+    wrow = iota((8, width), 0)
+    wlane = iota((8, width), 1)
+
+    def spread(part, b):
+        at = part * 8 + b
+        z, v, h = (gathered[f * 16 + at:f * 16 + at + 1] for f in range(3))
+        rows = jnp.where(in_pair == 1, v, jnp.where(in_pair == 2, h, z))
+        return jnp.where(row8 // 4 == b % 2, rows, 0.0)
+
+    for t in range(n_lev // 2):
+        sums = None
+        for b in (2 * t, 2 * t + 1):
+            re, im = spread(0, b), spread(1, b)
+            lhs = jnp.concatenate(
+                [
+                    jnp.concatenate([jnp.where(even_m, re, 0.0), jnp.where(even_m, 0.0, re), nothing, nothing], axis=0),
+                    jnp.concatenate([nothing, nothing, jnp.where(even_m, im, 0.0), jnp.where(even_m, 0.0, im)], axis=0),
+                ],
+                axis=1,
+            ).astype(BF16)
+            term = dot(lhs, tab[b], NT)
+            sums = term if sums is None else sums + term
+        ce, co, se, so = (sums[g * 8:(g + 1) * 8] for g in range(4))
+        p, q, s, d = ce + co, ce - co, se + so, se - so
+
+        def product(x):
+            return x * pltpu.roll(x, 7, 0)
+
+        p1, p2, p3, p4 = product(p + s), product(p - s), product(q - d), product(q + d)
+        count = jnp.where(wrow < 4, nlon[2 * t * n_wave + me], nlon[(2 * t + 1) * n_wave + me])
+        quarter = count // 4
+        share = jnp.where((wlane == 0) | (wlane == quarter), 0.5, 1.0)
+        share = jnp.where(wlane > quarter, 0.0, share)
+        a, e, f, g = (p1 + p2) * share, (p3 + p4) * share, (p1 - p2) * share, (p4 - p3) * share
+        folded = jnp.concatenate([a + e, a - e, f + g, f - g], axis=0).astype(BF16)
+        first = dot(folded, tab[2 * t], NN)
+        second = dot(folded, tab[2 * t + 1], NN)
+        row_n = jnp.where(row8 < 4, nlon[2 * t * n_wave + me], nlon[(2 * t + 1) * n_wave + me]).astype(F32)
+        row_w = jnp.where(row8 < 4, weights[2 * t * n_wave + me], weights[(2 * t + 1) * n_wave + me])
+        scale = 4.0 * (row_w / row_n)
+        parts = []
+        for part in range(2):
+            lanes = slice(part * LANE, (part + 1) * LANE)
+            both = [
+                jnp.where(even_m, x[part * 16:part * 16 + 8, lanes], x[part * 16 + 8:part * 16 + 16, lanes])
+                for x in (first, second)
+            ]
+            parts.append(jnp.where(row8 < 4, both[0], both[1]) * scale)
+        bsend[t * 16:(t + 1) * 16, :] = jnp.concatenate(parts, axis=0).astype(BF16)
+
+    for step in range(1, n_wave):
+        back_copy(step, me).start()
+    brecv[me] = bsend[...]
+    for step in range(1, n_wave):
+        back_copy(step, peer(n_wave - step)).wait_recv()
+
+    choose = jnp.where(lane16 == me * slots + row16, 1.0, 0.0).astype(BF16)
+    turned = dot(choose, brecv[...].reshape(depth, LANE), NT).astype(BF16)
+    placed = dot(turned, rmat[...], NN)
+    dcol = iota((slots, depth), 1)
+    own_pair = lax.rem(dcol // lats, slots // 2) == iota((slots, depth), 0) // 2
+    rows = jnp.concatenate(
+        [jnp.where(own_pair, placed[:, c * depth:(c + 1) * depth], 0.0) for c in range(cols)], axis=0
+    ).astype(BF16)
+    result = dot(rows, legp[...].reshape(depth, places * LANE), NN)
+    for k in range(blocks):
+        live = k * LANE + lane16 <= last
+        q = blocks - k
+        for c in range(cols):
+            even = result[c * slots:(c + 1) * slots, k * LANE:(k + 1) * LANE]
+            odd = result[c * slots:(c + 1) * slots, q * LANE:(q + 1) * LANE]
+            out[c, :, k * LANE:(k + 1) * LANE] = jnp.where(live, jnp.where(even_row, even, odd), 0.0)
+
+    for chunk in range(chunks):
+        lev_copy(lev, chunk, across, 0).wait_send()
+        lev_copy(lev, chunk, sibling, 1).wait_send()
+        lev_copy(across, chunk, sibling, 2).wait_send()
+    for step in range(1, n_wave):
+        four_copy(step, me).wait_send()
+        back_copy(step, me).wait_send()
+
+
+def fused(spectral, legendre, weights, nlon, assignment):
+    cols, slots, kmax = spectral.shape
+    lats = legendre.shape[1]
+    packed = kmax + LANE
+    depth = 4 * slots // 2 * lats
+    quarter = -(-(NLONPAD // 4 + 1) // LANE) * LANE
+    smem = pl.BlockSpec(memory_space=pltpu.SMEM)
+    vmem = pl.BlockSpec(memory_space=pltpu.VMEM)
+    dma = pltpu.SemaphoreType.DMA
+    return pl.pallas_call(
+        fused_kernel,
+        out_shape=jax.ShapeDtypeStruct((cols, slots, kmax), F32),
+        in_specs=[smem, smem, smem, vmem, vmem, vmem],
+        out_specs=vmem,
+        scratch_shapes=[
+            pltpu.VMEM((4, slots // 4, 2 * lats, packed), BF16),
+            pltpu.VMEM((cols, LANE, packed), BF16),
+            pltpu.VMEM((4, quarter, 2 * LANE), BF16),
+            pltpu.VMEM((depth, cols * depth), BF16),
+            pltpu.VMEM((8, 48, LANE), BF16),
+            pltpu.VMEM((8, 48, LANE), BF16),
+            pltpu.VMEM((32, LANE), BF16),
+            pltpu.VMEM((8, 32, LANE), BF16),
+            dma((3, slots // 4)),
+            dma((3, slots // 4)),
+            dma((8,)),
+            dma((8,)),
+            dma((8,)),
+            dma((8,)),
+        ],
+        compiler_params=pltpu.CompilerParams(
+            collective_id=0, has_side_effects=True, vmem_limit_bytes=48 * 1024 * 1024
+        ),
+    )(nlon, weights, assignment, assignment.reshape(1, -1), spectral, legendre)
+
+
 def solution(mesh):
+    def per_shard(spectral, legendre, weights, nlon, assignment):
+        fits = (
+            mesh.shape["wave"] == 8
+            and mesh.shape["lev"] == 4
+            and spectral.shape[:2] == (6, 16)
+            and legendre.shape[:2] == (16, 8)
+            and spectral.shape[2] == TRUNC + 1
+        )
+        plan = fused if fits else per_device
+        return plan(spectral, legendre, weights, nlon, assignment)
+
     return jax.shard_map(
-        per_device,
+        per_shard,
         mesh=mesh,
         in_specs=(P("lev", "wave", None), P("wave", "lev", None), P(), P(), P()),
         out_specs=P("lev", "wave", None),

time: 98.8 us -> 30.9 us (0.31)
  Pallas kernels: 0 us -> 27.4 us
  waiting for transfers between devices: 23.6 us -> 0 us
  other arithmetic: 22.7 us -> 0 us
  blocking collectives: 21.3 us -> 0 us
  between operations: 16 us -> 0.01 us
  starting transfers between devices: 5.84 us -> 0 us
  matrix products: 3.42 us -> 0 us
  local copies, waits for them, and re-layouts: 4.94 us -> 3.38 us
    pallas_call x0 -> x1, Pallas kernels: none -> 27.4 us  [fused(): pl.pallas_call(fused_kernel, out_shape=jax.ShapeDtypeStruct((cols, slots,...]
    reduce_scatter x1 -> x0, waiting for transfers between devices: 21.5 us -> none  [per_device(): lax.psum_scatter(band_term.astype(jnp.bfloat16), 'lev', scatter_dimension...]
    all_gather x1 -> x0, blocking collectives: 11.1 us -> none  [per_device(): spec_all = lax.all_gather(local, 'lev', axis=0, tiled=True)]
    all_to_all x1 -> x0, blocking collectives: 10.2 us -> none  [per_device(): lax.all_to_all(analysed, 'wave', split_axis=0, concat_axis=1, tiled=True)]
    lt x14 -> x0, other arithmetic: 8.18 us -> none  [compose_table(): usable = (lon_rows[:, None] < count) & (2 * waves[None, :] < count)]
    cos x7 -> x0, other arithmetic: 6.88 us -> none  [angle_parts(): return (jnp.cos(angle), jnp.sin(angle))]
    all_to_all x1 -> x0, starting transfers between devices: 5.81 us -> none  [per_device(): lax.all_to_all(four_local, 'wave', split_axis=1, concat_axis=0, tiled=True)]
    dot_general x16 -> x0, matrix products: 3.42 us -> none  [the longest x7 1.53 us: lon_block(): grid = 2.0 * jnp.dot(table, stacked, preferred_element_type=jnp.float32)]
  transfers between devices with their start and end apart: 2 -> 0, of which waited for: 2 -> 0; matrix products, arithmetic and copies ran while one was open for 2% -> 0% of each run, Pallas kernels for 0% -> 0%
where the time goes in v1:
time: 30.9 us; the launch traced here: 30.8 us
  Pallas kernels  27.4 us (89%)
  local copies, waits for them, and re-layouts  3.38 us (11%)
    pallas_call x1, Pallas kernels, fused(): pl.pallas_call(fused_kernel, out_shape=jax.ShapeDtypeStruct((cols, slots,...  27.4 us
    unnamed x11, local copies, waits for them, and re-layouts  3.38 us

profile of v1, /device:TPU:0, one launch (start us, length us, event | category | flops | bytes accessed | tf_op | source)
XLA Modules:
  0.0 30.8 jit_solution(4448853550051535316)
XLA Ops:
  0.0 0.0 copy-start.2
  0.0 0.0 copy-start.3
  0.0 0.0 copy-start.4
  0.0 0.6 %copy-done.2 = s32[128]{0:T(128)S(1)} copy-done((s32[128]{0:T(128)S(1)}, s32[128]{0:T(128)}, u32[]{:S(2)}) %copy-start.2) | copy-done | bytes 536
  0.7 0.0 copy-done.3
  0.7 0.0 copy-done.4
  0.7 0.0 copy-start
  0.7 1.0 %copy-done = bf16[16,8,1280]{2,1,0:T(8,128)(2,1)S(1)} copy-done((bf16[16,8,1280]{2,1,0:T(8,128)(2,1)S(1)}, bf16[16,8,1280]{2,1,0:T(8,128)(2,1)}, u32[]{:S(2)}) %copy-start) | copy-done | bytes 327704
  1.7 0.0 copy-start.1
  1.7 0.9 %copy-done.1 = bf16[6,16,1280]{2,1,0:T(8,128)(2,1)S(1)} copy-done((bf16[6,16,1280]{2,1,0:T(8,128)(2,1)S(1)}, bf16[6,16,1280]{2,1,0:T(8,128)(2,1)}, u32[]{:S(2)}) %copy-start.1) | copy-done | bytes 245784
  2.6 27.4 %shard_map.55 = f32[6,16,1280]{2,1,0:T(8,128)S(1)} custom-call(s32[32]{0:T(128)S(1)} %copy-done.3, f32[32]{0:T(128)S(1)} %copy-done.4, s32[128]{0:T(128)S(1)} %copy-done.2, s32[1,128]{1,0:T(1,128)S(1)} %bitcast.1, bf16[6,16,1280]{2,1,0:T(8,128)(2,1)S(1)} %copy-done.1, bf16[16,8,1280]{2,1,0:T(8,128)(2,1)S(1)} %copy-done), custom_call_target="tpu_custom_call" | custom-call | tf_op jit(solution)/shard_map/pallas_call | solution.py:413
  30.0 0.8 %copy.7 = f32[6,16,1280]{2,1,0:T(8,128)} copy(f32[6,16,1280]{2,1,0:T(8,128)S(1)} %shard_map.55) | data formatting | bytes 983040
Async XLA Ops:
  0.0 0.7 %copy-start.2 = (s32[128]{0:T(128)S(1)}, s32[128]{0:T(128)}, u32[]{:S(2)}) copy-start(s32[128]{0:T(128)} %waves_s.1) | copy-start | bytes 1540
  0.0 0.7 %copy-start.3 = (s32[32]{0:T(128)S(1)}, s32[32]{0:T(128)}, u32[]{:S(2)}) copy-start(s32[32]{0:T(128)} %nlon.1) | copy-start | bytes 388
  0.0 0.7 %copy-start.4 = (f32[32]{0:T(128)S(1)}, f32[32]{0:T(128)}, u32[]{:S(2)}) copy-start(f32[32]{0:T(128)} %weights.1) | copy-start | bytes 388
  0.7 1.0 %copy-start = (bf16[16,8,1280]{2,1,0:T(8,128)(2,1)S(1)}, bf16[16,8,1280]{2,1,0:T(8,128)(2,1)}, u32[]{:S(2)}) copy-start(bf16[16,8,1280]{2,1,0:T(8,128)(2,1)} %leg.1) | copy-start | bytes 983044
  1.7 0.9 %copy-start.1 = (bf16[6,16,1280]{2,1,0:T(8,128)(2,1)S(1)}, bf16[6,16,1280]{2,1,0:T(8,128)(2,1)}, u32[]{:S(2)}) copy-start(bf16[6,16,1280]{2,1,0:T(8,128)(2,1)} %spec.1) | copy-start | bytes 737284

commit v2 on v1

--- a/solution.py
+++ b/solution.py
@@ -119,16 +119,25 @@
 
 
 def fused_kernel(
-    nlon, weights, waves_s, waves_v, spec, leg, out,
-    legp, coefx, tab, rmat, fsend, frecv, bsend, brecv,
-    ag_send, ag_recv, f_ssem, f_rsem, b_ssem, b_rsem,
+    nlon_in, weights_in, waves_in, waves_row, spec_in, leg_in, out,
+    nlon, weights, waves_s, waves_v, spec, leg,
+    legp, coef, tab, rmat, emat, fsend, frecv, bsend, brecv,
+    in_sem, ag_send, ag_recv, f_ssem, f_rsem, b_ssem, b_rsem,
 ):
     n_wave, n_lev = 8, 4
+    chunks = leg.shape[0] // 4
+    moves = [
+        pltpu.make_async_copy(leg_in.at[pl.ds(4 * i, 4)], leg.at[pl.ds(4 * i, 4)], in_sem.at[i])
+        for i in range(chunks)
+    ]
+    small = ((waves_in, waves_s), (spec_in, spec), (waves_row, waves_v), (nlon_in, nlon), (weights_in, weights))
+    moves += [pltpu.make_async_copy(a, b, in_sem.at[chunks + i]) for i, (a, b) in enumerate(small)]
+    for move in [moves[chunks]] + moves[:chunks] + moves[chunks + 1:]:
+        move.start()
     cols, slots, kmax = spec.shape
     lats = leg.shape[1]
     blocks = kmax // LANE
     places = blocks + 1
-    chunks = slots // 4
     me = lax.axis_index("wave")
     lev = lax.axis_index("lev")
     sibling = lev + 1 - 2 * lax.rem(lev, 2)
@@ -154,11 +163,12 @@
             device_id_type=MESH,
         )
 
+    moves[chunks].wait()
     own = [waves_s[me * slots + s] for s in range(slots)]
 
     def pack_chunk(chunk):
         counts = [
-            (jnp.full((lats, LANE), TRUNC + 1, I32) - own[2 * i] + (LANE - 1)) // LANE
+            (jnp.full((lats, LANE), TRUNC + 1, I32) - own[2 * i] + (LANE - 1)) >> 7
             for i in (2 * chunk, 2 * chunk + 1)
         ]
         for p in range(places):
@@ -179,6 +189,7 @@
             legp[lev, chunk, :, p * LANE:(p + 1) * LANE] = jnp.concatenate(halves, axis=0).astype(BF16)
 
     for chunk in range(chunks):
+        moves[chunk].wait()
         pack_chunk(chunk)
         if chunk == 0:
             pl.semaphore_wait(barrier, n_wave - 1 + 2)
@@ -187,22 +198,26 @@
 
     row16 = iota((slots, LANE), 0)
     lane16 = iota((slots, LANE), 1)
-    even_row = lax.rem(row16, 2) == 0
+    even_row = row16 & 1 == 0
     last = jnp.zeros((slots, LANE), I32)
     for s in range(slots):
         last = jnp.where(row16 == s, TRUNC - own[s], last)
     zero16 = jnp.zeros((slots, LANE), F32)
-    coefx[...] = jnp.zeros(coefx.shape, BF16)
-    rows_at = pl.ds(pl.multiple_of(me * slots, slots), slots)
+    moves[chunks + 1].wait()
+    padding = jnp.zeros((LANE - cols * slots, LANE), F32)
     for p in range(places):
         q = blocks - p
         live = jnp.where(even_row, p * LANE, q * LANE) + lane16 <= last
+        pieces = []
         for c in range(cols):
             even = spec[c, :, p * LANE:(p + 1) * LANE].astype(F32) if p < blocks else zero16
             odd = spec[c, :, q * LANE:(q + 1) * LANE].astype(F32) if p > 0 else zero16
-            value = jnp.where(live, jnp.where(even_row, even, odd), 0.0)
-            coefx[c, rows_at, p * LANE:(p + 1) * LANE] = value.astype(BF16)
-
+            pieces.append(jnp.where(live, jnp.where(even_row, even, odd), 0.0))
+        piece = jnp.concatenate(pieces + [padding], axis=0)
+        coef[p * LANE:(p + 1) * LANE, :] = piece.T.astype(BF16)
+
+    for move in moves[chunks + 2:]:
+        move.wait()
     waves = waves_v[...]
     waves_f = waves.astype(F32)
 
@@ -244,30 +259,36 @@
     depth = n_lev * slots // 2 * lats
     rrow = iota((depth, depth), 0)
     rcol = iota((depth, depth), 1)
-    band_c = rcol // (slots // 2 * lats)
-    same = (rrow // 32) == lax.rem(rcol, lats)
-    base = (band_c // 2) * 16 + lax.rem(band_c, 2) * 4
+    band_c = rcol >> 6
+    same = (rrow >> 5) == rcol & 7
+    base = (band_c >> 1) * 16 + (band_c & 1) * 4
     for c in range(cols):
-        hit = same & (lax.rem(rrow, 32) == base + (c % 2) * 8 + (2 - c // 2))
+        hit = same & (rrow & 31 == base + (c % 2) * 8 + (2 - c // 2))
         rmat[:, c * depth:(c + 1) * depth] = jnp.where(hit, 1.0, 0.0).astype(BF16)
 
+    erow = iota((LANE, cols * LANE), 0)
+    ecol = iota((LANE, cols * LANE), 1)
+    lane_of = ecol & (LANE - 1)
+    hit = erow == (ecol >> 7) * slots + (lane_of & (slots - 1))
+    emat[...] = jnp.where(hit, 1.0, 0.0).astype(BF16)
+
+    krow, kcol = iota((LANE, LANE), 0), iota((LANE, LANE), 1)
+    shift = jnp.where((krow < 32) & (kcol == krow + 32 * lax.rem(me, 4)), 1.0, 0.0).astype(BF16)
+
     half = slots // 2 * lats
-    coef_all = coefx[...].reshape(cols * LANE, places * LANE)
-    yrow = iota((half, LANE), 0) // lats
+    coef_all = coef[...]
+    yrow = iota((half, LANE), 0) >> 3
     ylane = iota((half, LANE), 1)
-    mine = (ylane // slots == me) & (lax.rem(ylane, slots) // 2 == yrow)
+    mine = (ylane & (slots - 1)) >> 1 == yrow
     srow = iota((n_wave * 8, half), 0)
     scol = iota((n_wave * 8, half), 1)
-    same_lat = srow // 8 == lax.rem(scol, lats)
+    same_lat = srow >> 3 == scol & 7
 
     def synth(band):
         packed = legp[band].reshape(half, places * LANE)
-        four = dot(packed, coef_all, NT)
-        pick = jnp.where(same_lat & (lax.rem(srow, 8) == band), 1.0, 0.0).astype(BF16)
-        parts = [
-            jnp.where(mine, four[:, c * LANE:(c + 1) * LANE], 0.0).astype(BF16) for c in range(cols)
-        ]
-        return dot(pick, jnp.concatenate(parts, axis=1), NN)
+        four = jnp.where(mine, dot(packed, coef_all, NN), 0.0).astype(BF16)
+        pick = jnp.where(same_lat & (srow & 7 == band), 1.0, 0.0).astype(BF16)
+        return dot(pick, four, NN)
 
     total = synth(lev)
     for chunk in range(chunks):
@@ -278,14 +299,7 @@
         lev_copy(far, chunk, sibling, 2).wait_recv()
     total = total + synth(far)
     for j in range(n_wave):
-        for f in range(cols // 2):
-            fsend[j, f * 16:(f + 1) * 16, :] = jnp.concatenate(
-                [
-                    total[j * 8:(j + 1) * 8, (2 * f) * LANE:(2 * f + 1) * LANE],
-                    total[j * 8:(j + 1) * 8, (2 * f + 1) * LANE:(2 * f + 2) * LANE],
-                ],
-                axis=0,
-            ).astype(BF16)
+        fsend[j] = total[j * 8:(j + 1) * 8]
 
     def four_copy(step, slot):
         return pltpu.make_async_remote_copy(
@@ -299,7 +313,7 @@
 
     def back_copy(step, slot):
         return pltpu.make_async_remote_copy(
-            src_ref=bsend,
+            src_ref=bsend.at[peer(step)],
             dst_ref=brecv.at[slot],
             send_sem=b_ssem.at[step],
             recv_sem=b_rsem.at[step],
@@ -313,21 +327,28 @@
     for step in range(1, n_wave):
         four_copy(step, peer(n_wave - step)).wait_recv()
 
-    gathered = jnp.sum(frecv[...].astype(F32), axis=0)
-    even_m = lax.rem(waves, 2) == 0
+    wide = dot(frecv[...].reshape(n_wave * 8, LANE).astype(BF16), emat[...], NN)
+    from_wave = iota((8, LANE), 1) >> 4
+    columns = []
+    for c in range(cols):
+        part = wide[0:8, c * LANE:(c + 1) * LANE]
+        for j in range(1, n_wave):
+            part = jnp.where(from_wave == j, wide[j * 8:(j + 1) * 8, c * LANE:(c + 1) * LANE], part)
+        columns.append(part)
+    even_m = waves & 1 == 0
     row8 = iota((8, LANE), 0)
-    in_pair = lax.rem(row8, 4)
+    in_pair = row8 & 3
     nothing = jnp.zeros((8, LANE), F32)
     width = tab.shape[1]
     wrow = iota((8, width), 0)
     wlane = iota((8, width), 1)
 
     def spread(part, b):
-        at = part * 8 + b
-        z, v, h = (gathered[f * 16 + at:f * 16 + at + 1] for f in range(3))
+        z, v, h = (columns[2 * f + part][b:b + 1] for f in range(3))
         rows = jnp.where(in_pair == 1, v, jnp.where(in_pair == 2, h, z))
-        return jnp.where(row8 // 4 == b % 2, rows, 0.0)
-
+        return jnp.where(row8 >> 2 == b % 2, rows, 0.0)
+
+    back = []
     for t in range(n_lev // 2):
         sums = None
         for b in (2 * t, 2 * t + 1):
@@ -349,7 +370,7 @@
 
         p1, p2, p3, p4 = product(p + s), product(p - s), product(q - d), product(q + d)
         count = jnp.where(wrow < 4, nlon[2 * t * n_wave + me], nlon[(2 * t + 1) * n_wave + me])
-        quarter = count // 4
+        quarter = count >> 2
         share = jnp.where((wlane == 0) | (wlane == quarter), 0.5, 1.0)
         share = jnp.where(wlane > quarter, 0.0, share)
         a, e, f, g = (p1 + p2) * share, (p3 + p4) * share, (p1 - p2) * share, (p4 - p3) * share
@@ -367,19 +388,23 @@
                 for x in (first, second)
             ]
             parts.append(jnp.where(row8 < 4, both[0], both[1]) * scale)
-        bsend[t * 16:(t + 1) * 16, :] = jnp.concatenate(parts, axis=0).astype(BF16)
-
+        back += parts
+
+    rows = jnp.concatenate(back + [jnp.zeros((LANE - 32, LANE), F32)], axis=0)
+    bsend[...] = dot(rows.T.astype(BF16), shift, NN).astype(BF16).reshape(n_wave, slots, LANE)
     for step in range(1, n_wave):
         back_copy(step, me).start()
-    brecv[me] = bsend[...]
+    brecv[me] = bsend[me]
     for step in range(1, n_wave):
         back_copy(step, peer(n_wave - step)).wait_recv()
 
-    choose = jnp.where(lane16 == me * slots + row16, 1.0, 0.0).astype(BF16)
-    turned = dot(choose, brecv[...].reshape(depth, LANE), NT).astype(BF16)
+    arrived = brecv[...].astype(F32)
+    turned = jnp.concatenate(
+        [sum(arrived[4 * g + j] for j in range(4)) for g in range(2)], axis=1
+    ).astype(BF16)
     placed = dot(turned, rmat[...], NN)
     dcol = iota((slots, depth), 1)
-    own_pair = lax.rem(dcol // lats, slots // 2) == iota((slots, depth), 0) // 2
+    own_pair = (dcol >> 3) & 7 == iota((slots, depth), 0) >> 1
     rows = jnp.concatenate(
         [jnp.where(own_pair, placed[:, c * depth:(c + 1) * depth], 0.0) for c in range(cols)], axis=0
     ).astype(BF16)
@@ -407,23 +432,30 @@
     packed = kmax + LANE
     depth = 4 * slots // 2 * lats
     quarter = -(-(NLONPAD // 4 + 1) // LANE) * LANE
-    smem = pl.BlockSpec(memory_space=pltpu.SMEM)
     vmem = pl.BlockSpec(memory_space=pltpu.VMEM)
     dma = pltpu.SemaphoreType.DMA
     return pl.pallas_call(
         fused_kernel,
         out_shape=jax.ShapeDtypeStruct((cols, slots, kmax), F32),
-        in_specs=[smem, smem, smem, vmem, vmem, vmem],
+        in_specs=[pl.BlockSpec(memory_space=pltpu.HBM)] * 6,
         out_specs=vmem,
         scratch_shapes=[
+            pltpu.SMEM(nlon.shape, I32),
+            pltpu.SMEM(weights.shape, F32),
+            pltpu.SMEM(assignment.shape, I32),
+            pltpu.VMEM((1, assignment.shape[0]), I32),
+            pltpu.VMEM(spectral.shape, BF16),
+            pltpu.VMEM(legendre.shape, BF16),
             pltpu.VMEM((4, slots // 4, 2 * lats, packed), BF16),
-            pltpu.VMEM((cols, LANE, packed), BF16),
+            pltpu.VMEM((packed, LANE), BF16),
             pltpu.VMEM((4, quarter, 2 * LANE), BF16),
             pltpu.VMEM((depth, cols * depth), BF16),
-            pltpu.VMEM((8, 48, LANE), BF16),
-            pltpu.VMEM((8, 48, LANE), BF16),
-            pltpu.VMEM((32, LANE), BF16),
-            pltpu.VMEM((8, 32, LANE), BF16),
+            pltpu.VMEM((LANE, cols * LANE), BF16),
+            pltpu.VMEM((8, 8, LANE), F32),
+            pltpu.VMEM((8, 8, LANE), F32),
+            pltpu.VMEM((8, slots, LANE), BF16),
+            pltpu.VMEM((8, slots, LANE), BF16),
+            dma((slots // 4 + 5,)),
             dma((3, slots // 4)),
             dma((3, slots // 4)),
             dma((8,)),
@@ -432,7 +464,7 @@
             dma((8,)),
         ],
         compiler_params=pltpu.CompilerParams(
-            collective_id=0, has_side_effects=True, vmem_limit_bytes=48 * 1024 * 1024
+            collective_id=0, has_side_effects=True, vmem_limit_bytes=60 * 1024 * 1024
         ),
     )(nlon, weights, assignment, assignment.reshape(1, -1), spectral, legendre)
 

time: 30.9 us -> 26.5 us (0.86)
  Pallas kernels: 27.4 us -> 24.5 us
  local copies, waits for them, and re-layouts: 3.38 us -> 1.84 us
    pallas_call x1, Pallas kernels: 27.4 us -> 24.5 us  [fused(): pl.pallas_call(fused_kernel, out_shape=jax.ShapeDtypeStruct((cols, slots,...]
    unnamed x11 -> x1, local copies, waits for them, and re-layouts: 3.38 us -> 1.84 us
where the time goes in v2:
time: 26.5 us; the launch traced here: 26.4 us
  Pallas kernels  24.5 us (92%)
  local copies, waits for them, and re-layouts  1.84 us (7%)
    pallas_call x1, Pallas kernels, fused(): pl.pallas_call(fused_kernel, out_shape=jax.ShapeDtypeStruct((cols, slots,...  24.5 us
    unnamed x1, local copies, waits for them, and re-layouts  1.84 us

profile of v2, /device:TPU:0, one launch (start us, length us, event | category | flops | bytes accessed | tf_op | source)
XLA Modules:
  0.0 26.4 jit_solution(14423649367032752749)
XLA Ops:
  0.0 24.5 %shard_map.55 = f32[6,16,1280]{2,1,0:T(8,128)} custom-call(s32[32]{0:T(128)} %nlon_in.1, f32[32]{0:T(128)} %weights_in.1, s32[128]{0:T(128)} %waves_in.1, s32[1,128]{1,0:T(1,128)} %bitcast.1, bf16[6,16,1280]{2,1,0:T(8,128)(2,1)} %spec_in.1, bf16[16,8,1280]{2,1,0:T(8,128)(2,1)} %leg_in.1), custom_call_target="tpu_custom_call" | custom-call | tf_op jit(solution)/shard_map/pallas_call | solution.py:437
  24.5 1.8 %copy.7 = f32[6,16,1280]{2,1,0:T(8,128)} copy(f32[6,16,1280]{2,1,0:T(8,128)} %shard_map.55) | data formatting | bytes 983040

commit v3 on v2

--- a/solution.py
+++ b/solution.py
@@ -125,6 +125,7 @@
     in_sem, ag_send, ag_recv, f_ssem, f_rsem, b_ssem, b_rsem,
 ):
     n_wave, n_lev = 8, 4
+    far_first = (6, 2, 7, 1, 5, 3, 4)
     chunks = leg.shape[0] // 4
     moves = [
         pltpu.make_async_copy(leg_in.at[pl.ds(4 * i, 4)], leg.at[pl.ds(4 * i, 4)], in_sem.at[i])
@@ -252,9 +253,13 @@
             tab[b, t * LANE:(t + 1) * LANE, 0:LANE] = (cq * fine_cos - sq * fine_sin).astype(BF16)
             tab[b, t * LANE:(t + 1) * LANE, LANE:2 * LANE] = (-(sq * fine_cos + cq * fine_sin)).astype(BF16)
 
-    for b in range(n_lev):
-        tables(b)
-        forward(b)
+    tables(0)
+    forward(0)
+    tables(1)
+    forward(1)
+    tables(2)
+    tables(3)
+    forward(2)
 
     depth = n_lev * slots // 2 * lats
     rrow = iota((depth, depth), 0)
@@ -294,6 +299,7 @@
     for chunk in range(chunks):
         lev_copy(sibling, chunk, sibling, 1).wait_recv()
     total = total + synth(sibling)
+    forward(3)
     total = total + synth(across)
     for chunk in range(chunks):
         lev_copy(far, chunk, sibling, 2).wait_recv()
@@ -321,7 +327,7 @@
             device_id_type=MESH,
         )
 
-    for step in range(1, n_wave):
+    for step in far_first:
         four_copy(step, me).start()
     frecv[me] = fsend[me]
     for step in range(1, n_wave):
@@ -392,7 +398,7 @@
 
     rows = jnp.concatenate(back + [jnp.zeros((LANE - 32, LANE), F32)], axis=0)
     bsend[...] = dot(rows.T.astype(BF16), shift, NN).astype(BF16).reshape(n_wave, slots, LANE)
-    for step in range(1, n_wave):
+    for step in far_first:
         back_copy(step, me).start()
     brecv[me] = bsend[me]
     for step in range(1, n_wave):
@@ -436,7 +442,7 @@
     dma = pltpu.SemaphoreType.DMA
     return pl.pallas_call(
         fused_kernel,
-        out_shape=jax.ShapeDtypeStruct((cols, slots, kmax), F32),
+        out_shape=pltpu.VMEM((cols, slots, kmax), F32),
         in_specs=[pl.BlockSpec(memory_space=pltpu.HBM)] * 6,
         out_specs=vmem,
         scratch_shapes=[
@@ -464,7 +470,7 @@
             dma((8,)),
         ],
         compiler_params=pltpu.CompilerParams(
-            collective_id=0, has_side_effects=True, vmem_limit_bytes=60 * 1024 * 1024
+            collective_id=0, has_side_effects=True, vmem_limit_bytes=56 * 1024 * 1024
         ),
     )(nlon, weights, assignment, assignment.reshape(1, -1), spectral, legendre)
 

time: 26.5 us -> 24.3 us (0.917)
  Pallas kernels: 24.5 us -> 23.4 us
  local copies, waits for them, and re-layouts: 1.84 us -> 0.78 us
    pallas_call x1, Pallas kernels: 24.5 us -> 23.4 us  [fused(): pl.pallas_call(fused_kernel, out_shape=pltpu.VMEM((cols, slots, kmax), F3...]
    unnamed x1, local copies, waits for them, and re-layouts: 1.84 us -> 0.78 us
where the time goes in v3:
time: 24.3 us; the launch traced here: 24.2 us
  Pallas kernels  23.4 us (96%)
  local copies, waits for them, and re-layouts  0.78 us (3%)
    pallas_call x1, Pallas kernels, fused(): pl.pallas_call(fused_kernel, out_shape=pltpu.VMEM((cols, slots, kmax), F3...  23.4 us
    unnamed x1, local copies, waits for them, and re-layouts  0.78 us

profile of v3, /device:TPU:0, one launch (start us, length us, event | category | flops | bytes accessed | tf_op | source)
XLA Modules:
  0.0 24.2 jit_solution(4401378313219138378)
XLA Ops:
  0.0 23.4 %shard_map.55 = f32[6,16,1280]{2,1,0:T(8,128)S(1)} custom-call(s32[32]{0:T(128)} %nlon_in.1, f32[32]{0:T(128)} %weights_in.1, s32[128]{0:T(128)} %waves_in.1, s32[1,128]{1,0:T(1,128)} %bitcast.1, bf16[6,16,1280]{2,1,0:T(8,128)(2,1)} %spec_in.1, bf16[16,8,1280]{2,1,0:T(8,128)(2,1)} %leg_in.1), custom_call_target="tpu_custom_call" | custom-call | tf_op jit(solution)/shard_map/pallas_call | solution.py:443
  23.4 0.8 %copy.7 = f32[6,16,1280]{2,1,0:T(8,128)} copy(f32[6,16,1280]{2,1,0:T(8,128)S(1)} %shard_map.55) | data formatting | bytes 983040

commit v4 on v3

--- a/solution.py
+++ b/solution.py
@@ -122,7 +122,7 @@
     nlon_in, weights_in, waves_in, waves_row, spec_in, leg_in, out,
     nlon, weights, waves_s, waves_v, spec, leg,
     legp, coef, tab, rmat, emat, fsend, frecv, bsend, brecv,
-    in_sem, ag_send, ag_recv, f_ssem, f_rsem, b_ssem, b_rsem,
+    in_sem, ag_send, ag_recv, f_ssem, f_rsem, b_ssem, b_rsem, met,
 ):
     n_wave, n_lev = 8, 4
     far_first = (6, 2, 7, 1, 5, 3, 4)
@@ -148,11 +148,20 @@
     def peer(step):
         return lax.rem(me + step, n_wave)
 
+    partners = (me + 1 - 2 * lax.rem(me, 2), me + 2 - 4 * lax.rem(me // 2, 2), lax.rem(me + 4, n_wave))
     barrier = pltpu.get_barrier_semaphore()
-    for step in range(1, n_wave):
-        pl.semaphore_signal(barrier, inc=1, device_id=(peer(step), lev), device_id_type=MESH)
     for other in (sibling, across):
         pl.semaphore_signal(barrier, inc=1, device_id=(me, other), device_id_type=MESH)
+    for partner in partners:
+        pl.semaphore_signal(barrier, inc=1, device_id=(partner, lev), device_id_type=MESH)
+
+    def greet(turn):
+        for axis, partner in enumerate(partners):
+            pl.semaphore_signal(met.at[turn, axis], inc=1, device_id=(partner, lev), device_id_type=MESH)
+
+    def met_all(turn):
+        for axis in range(len(partners)):
+            pl.semaphore_wait(met.at[turn, axis], 1)
 
     def lev_copy(band, chunk, target, sem):
         return pltpu.make_async_remote_copy(
@@ -193,9 +202,11 @@
         moves[chunk].wait()
         pack_chunk(chunk)
         if chunk == 0:
-            pl.semaphore_wait(barrier, n_wave - 1 + 2)
+            pl.semaphore_wait(barrier, 2 + len(partners))
         lev_copy(lev, chunk, across, 0).start()
         lev_copy(lev, chunk, sibling, 1).start()
+        if chunk == 0:
+            greet(0)
 
     row16 = iota((slots, LANE), 0)
     lane16 = iota((slots, LANE), 1)
@@ -255,6 +266,8 @@
 
     tables(0)
     forward(0)
+    met_all(0)
+    greet(1)
     tables(1)
     forward(1)
     tables(2)
@@ -327,6 +340,7 @@
             device_id_type=MESH,
         )
 
+    met_all(1)
     for step in far_first:
         four_copy(step, me).start()
     frecv[me] = fsend[me]
@@ -468,6 +482,7 @@
             dma((8,)),
             dma((8,)),
             dma((8,)),
+            pltpu.SemaphoreType.REGULAR((2, 3)),
         ],
         compiler_params=pltpu.CompilerParams(
             collective_id=0, has_side_effects=True, vmem_limit_bytes=56 * 1024 * 1024

time: 24.3 us -> 23 us (0.947)
  Pallas kernels: 23.4 us -> 22.1 us
    pallas_call x1, Pallas kernels: 23.4 us -> 22.1 us  [fused(): pl.pallas_call(fused_kernel, out_shape=pltpu.VMEM((cols, slots, kmax), F3...]
where the time goes in v4:
time: 23 us; the launch traced here: 22.9 us
  Pallas kernels  22.1 us (96%)
  local copies, waits for them, and re-layouts  0.78 us (3%)
    pallas_call x1, Pallas kernels, fused(): pl.pallas_call(fused_kernel, out_shape=pltpu.VMEM((cols, slots, kmax), F3...  22.1 us
    unnamed x1, local copies, waits for them, and re-layouts  0.78 us

profile of v4, /device:TPU:0, one launch (start us, length us, event | category | flops | bytes accessed | tf_op | source)
XLA Modules:
  0.0 22.9 jit_solution(4820577692353878902)
XLA Ops:
  0.0 22.1 %shard_map.55 = f32[6,16,1280]{2,1,0:T(8,128)S(1)} custom-call(s32[32]{0:T(128)} %nlon_in.1, f32[32]{0:T(128)} %weights_in.1, s32[128]{0:T(128)} %waves_in.1, s32[1,128]{1,0:T(1,128)} %bitcast.1, bf16[6,16,1280]{2,1,0:T(8,128)(2,1)} %spec_in.1, bf16[16,8,1280]{2,1,0:T(8,128)(2,1)} %leg_in.1), custom_call_target="tpu_custom_call" | custom-call | tf_op jit(solution)/shard_map/pallas_call | solution.py:457
  22.1 0.8 %copy.7 = f32[6,16,1280]{2,1,0:T(8,128)} copy(f32[6,16,1280]{2,1,0:T(8,128)S(1)} %shard_map.55) | data formatting | bytes 983040
